TPU v7x, 128 devices: a whole 4x4x4 slice. The times are simulated.
128 devices in a mesh: rep: 64 (over x, z, y_lo, core), shard: 2 (over y_hi).
Axes of the slice: x: 4, y: 4 (y_hi: 2, y_lo: 2; y = y_hi * 2 + y_lo), z: 4, core: 2. Of those that a mesh axis runs over, the one named last changes fastest.
Arguments:
- tokens: bfloat16 [32768, 768], P(('rep', 'shard')), may hold values from -6 to 6
- w_qkv: bfloat16 [768, 2304], P('shard'), may hold values from -0.21875 to 0.21875
- b_qv: bfloat16 [1536], P('shard'), may hold values from -3 to 3
- w_out: bfloat16 [768, 768], P('shard'), may hold values from -0.875 to 0.875
- b_out: bfloat16 [768], P('shard'), may hold values from -3 to 3
- w_up: bfloat16 [768, 3072], P('shard'), may hold values from -0.21875 to 0.21875
- b_up: bfloat16 [3072], P('shard'), may hold values from -3 to 3
- w_down: bfloat16 [3072, 768], P('shard'), may hold values from -0.109375 to 0.109375
- b_down: bfloat16 [768], P('shard'), may hold values from -3 to 3
- gain_one: bfloat16 [768], P('shard'), may hold values from 0.5 to 1.5
- shift_one: bfloat16 [768], P('shard'), may hold values from -2 to 2
- gain_two: bfloat16 [768], P('shard'), may hold values from 0.5 to 1.5
- shift_two: bfloat16 [768], P('shard'), may hold values from -2 to 2
- cotangent: bfloat16 [32768, 768], P(('rep', 'shard')), may hold values from -6 to 6
Outputs:
- result: bfloat16 [32768, 768], P(('rep', 'shard'))
- input_grad: float32 [32768, 768], P(('rep', 'shard'))
- grad_w_qkv: float32 [768, 2304], P('shard')
- grad_b_qv: float32 [1536], P('shard')
- grad_w_out: float32 [768, 768], P('shard')
- grad_b_out: float32 [768], P('shard')
- grad_w_up: float32 [768, 3072], P('shard')
- grad_b_up: float32 [3072], P('shard')
- grad_w_down: float32 [3072, 768], P('shard')
- grad_b_down: float32 [768], P('shard')
- grad_gain_one: float32 [768], P('shard')
- grad_shift_one: float32 [768], P('shard')
- grad_gain_two: float32 [768], P('shard')
- grad_shift_two: float32 [768], P('shard')
All inputs are finite; a program needn't handle non-finite values.
Results may differ from a plain program's by a relative error of at most 0.014.
Values may be sent and summed in bfloat16 or wider, within the bound.
No kernel may reach another device: no remote copies, remote signals or barrier semaphores. Data moves between devices by JAX's collectives and lax.ppermute only.
A program may use at most 128 MiB of HBM per device.

v0:
```python
import jax
import jax.numpy as jnp
from jax import lax
from jax.sharding import PartitionSpec as P

HEAD_DIM = 64


eps = 1e-05


def shifted(value, axis, steps):
    count = lax.axis_size(axis)
    leading, last = (max(0, -steps), min(count, count - steps))
    return lax.ppermute(value, axis, [(source, source + steps) for source in range(leading, last)])


def layer_norm(values, gain, shift):
    center = jnp.mean(values, axis=-1, keepdims=True)
    centered = values - center
    spread = jnp.mean(centered * centered, axis=-1, keepdims=True)
    return centered * lax.rsqrt(spread + eps) * gain + shift


def contract_rows(left, right):
    return lax.dot_general(
        left, right, (((0,), (0,)), ((), ())), preferred_element_type=jnp.float32
    )


def contract_cols(left, right):
    return lax.dot_general(
        left, right, (((1,), (1,)), ((), ())), preferred_element_type=jnp.float32
    )


def on_device(
    tokens,
    w_qkv,
    b_qv,
    w_out,
    b_out,
    w_up,
    b_up,
    w_down,
    b_down,
    gain_one,
    shift_one,
    gain_two,
    shift_two,
    cotangent,
):
    gathered = (
        lax.all_gather(w_qkv, "shard", axis=0, tiled=True),
        lax.all_gather(b_qv, "shard", axis=0, tiled=True),
        lax.all_gather(w_out, "shard", axis=0, tiled=True),
        lax.all_gather(b_out, "shard", axis=0, tiled=True),
        lax.all_gather(w_up, "shard", axis=0, tiled=True),
        lax.all_gather(b_up, "shard", axis=0, tiled=True),
        lax.all_gather(w_down, "shard", axis=0, tiled=True),
        lax.all_gather(b_down, "shard", axis=0, tiled=True),
        lax.all_gather(gain_one, "shard", axis=0, tiled=True),
        lax.all_gather(shift_one, "shard", axis=0, tiled=True),
        lax.all_gather(gain_two, "shard", axis=0, tiled=True),
        lax.all_gather(shift_two, "shard", axis=0, tiled=True),
    )
    rows = tokens.shape[0]
    width = tokens.shape[1]
    heads = width // HEAD_DIM
    floats = tokens.astype(jnp.float32)
    bias_qv = gathered[1].astype(jnp.float32)
    normed, norm_one_back = jax.vjp(
        layer_norm, floats, gathered[8].astype(jnp.float32), gathered[9].astype(jnp.float32)
    )
    normed_low = normed.astype(jnp.bfloat16)
    projected = jnp.dot(normed_low, gathered[0], preferred_element_type=jnp.float32)
    queries = ((projected[:, :width] + bias_qv[:width]) * 0.125).astype(jnp.bfloat16)
    keys_here = projected[:, width : 2 * width].astype(jnp.bfloat16)
    values_here = (projected[:, 2 * width :] + bias_qv[width:]).astype(jnp.bfloat16)
    pairs_here = jnp.concatenate([keys_here, values_here], axis=1)
    pairs_prev = shifted(pairs_here, "shard", 1)
    pairs_all = jnp.concatenate([pairs_prev, pairs_here], axis=0)
    keys_heads = jnp.transpose(pairs_all[:, :width].reshape(2 * rows, heads, HEAD_DIM), (1, 0, 2))
    values_heads = jnp.transpose(pairs_all[:, width:].reshape(2 * rows, heads, HEAD_DIM), (1, 0, 2))
    query_heads = jnp.transpose(queries.reshape(rows, heads, HEAD_DIM), (1, 0, 2))
    position = lax.axis_index("shard")
    query_place = position * rows + jnp.arange(rows)
    key_place = (position - 1) * rows + jnp.arange(2 * rows)
    allowed = (key_place[None, :] <= query_place[:, None]) & (key_place[None, :] >= 0)

    def score_block(query_one, key_one):
        raw = lax.dot_general(
            query_one, key_one, (((1,), (1,)), ((), ())), preferred_element_type=jnp.float32
        )
        return jnp.where(allowed, raw, -1e30)

    def head_forward(inputs):
        query_one, key_one, value_one = inputs
        scores = score_block(query_one, key_one)
        top_score = jnp.max(scores, axis=-1, keepdims=True)
        expo = jnp.exp(scores - top_score)
        total = jnp.sum(expo, axis=-1, keepdims=True)
        weights_low = (expo / total).astype(jnp.bfloat16)
        attended_one = jnp.dot(weights_low, value_one, preferred_element_type=jnp.float32)
        return (attended_one, top_score + jnp.log(total))

    attended_heads, log_total = lax.map(head_forward, (query_heads, keys_heads, values_heads))
    attended = jnp.transpose(attended_heads, (1, 0, 2)).reshape(rows, width)
    attended_low = attended.astype(jnp.bfloat16)
    branch = jnp.dot(attended_low, gathered[2], preferred_element_type=jnp.float32) + gathered[
        3
    ].astype(jnp.float32)
    middle = floats + branch
    normed_two, norm_two_back = jax.vjp(
        layer_norm, middle, gathered[10].astype(jnp.float32), gathered[11].astype(jnp.float32)
    )
    normed_two_low = normed_two.astype(jnp.bfloat16)
    hidden = jnp.dot(normed_two_low, gathered[4], preferred_element_type=jnp.float32) + gathered[
        5
    ].astype(jnp.float32)
    activated, gelu_back = jax.vjp(jax.nn.gelu, hidden)
    activated_low = activated.astype(jnp.bfloat16)
    out_branch = jnp.dot(activated_low, gathered[6], preferred_element_type=jnp.float32) + gathered[
        7
    ].astype(jnp.float32)
    result = (middle + out_branch).astype(jnp.bfloat16)
    again = (
        lax.all_gather(w_qkv, "shard", axis=0, tiled=True),
        lax.all_gather(b_qv, "shard", axis=0, tiled=True),
        lax.all_gather(w_out, "shard", axis=0, tiled=True),
        lax.all_gather(b_out, "shard", axis=0, tiled=True),
        lax.all_gather(w_up, "shard", axis=0, tiled=True),
        lax.all_gather(b_up, "shard", axis=0, tiled=True),
        lax.all_gather(w_down, "shard", axis=0, tiled=True),
        lax.all_gather(b_down, "shard", axis=0, tiled=True),
        lax.all_gather(gain_one, "shard", axis=0, tiled=True),
        lax.all_gather(shift_one, "shard", axis=0, tiled=True),
        lax.all_gather(gain_two, "shard", axis=0, tiled=True),
        lax.all_gather(shift_two, "shard", axis=0, tiled=True),
    )
    grad_final = cotangent.astype(jnp.float32)
    grad_wdown = contract_rows(activated_low, cotangent)
    grad_bdown = jnp.sum(cotangent, axis=0, dtype=jnp.float32)
    grad_act = contract_cols(cotangent, again[6])
    (grad_hidden,) = gelu_back(grad_act)
    grad_hidden_low = grad_hidden.astype(jnp.bfloat16)
    grad_wup = contract_rows(normed_two_low, grad_hidden_low)
    grad_bup = jnp.sum(grad_hidden_low, axis=0, dtype=jnp.float32)
    grad_norm_two = contract_cols(grad_hidden_low, again[4])
    grad_mid_norm, grad_gtwo, grad_stwo = norm_two_back(grad_norm_two)
    grad_middle = grad_final + grad_mid_norm
    grad_branch_low = grad_middle.astype(jnp.bfloat16)
    grad_wout = contract_rows(attended_low, grad_branch_low)
    grad_bout = jnp.sum(grad_branch_low, axis=0, dtype=jnp.float32)
    grad_att = contract_cols(grad_branch_low, again[2]).astype(jnp.bfloat16)
    grad_att_heads = jnp.transpose(grad_att.reshape(rows, heads, HEAD_DIM), (1, 0, 2))

    def head_backward(inputs):
        query_one, key_one, value_one, grad_one, log_one = inputs
        probs = jnp.exp(score_block(query_one, key_one) - log_one)
        probs_low = probs.astype(jnp.bfloat16)
        grad_probs = lax.dot_general(
            grad_one, value_one, (((1,), (1,)), ((), ())), preferred_element_type=jnp.float32
        )
        grad_values_one = contract_rows(probs_low, grad_one)
        inner = jnp.sum(probs * grad_probs, axis=-1, keepdims=True)
        grad_scores_low = (probs * (grad_probs - inner)).astype(jnp.bfloat16)
        grad_queries_one = jnp.dot(grad_scores_low, key_one, preferred_element_type=jnp.float32)
        grad_keys_one = contract_rows(grad_scores_low, query_one)
        return (grad_queries_one, grad_keys_one, grad_values_one)

    grad_q_heads, grad_k_heads, grad_v_heads = lax.map(
        head_backward, (query_heads, keys_heads, values_heads, grad_att_heads, log_total)
    )
    grad_queries = jnp.transpose(grad_q_heads, (1, 0, 2)).reshape(rows, width)
    grad_keys = jnp.transpose(grad_k_heads, (1, 0, 2)).reshape(2 * rows, width)
    grad_values = jnp.transpose(grad_v_heads, (1, 0, 2)).reshape(2 * rows, width)
    grad_pairs = jnp.concatenate([grad_keys, grad_values], axis=1)
    returned = shifted(grad_pairs[:rows].astype(jnp.bfloat16), "shard", -1).astype(jnp.float32)
    pair_grads = grad_pairs[rows:] + returned
    grad_proj_low = jnp.concatenate(
        [grad_queries.astype(jnp.bfloat16) * 0.125, pair_grads.astype(jnp.bfloat16)], axis=1
    )
    grad_wqkv = contract_rows(normed_low, grad_proj_low)
    column_sums = jnp.sum(grad_proj_low, axis=0, dtype=jnp.float32)
    grad_bqv = jnp.concatenate([column_sums[:width], column_sums[2 * width :]])
    grad_norm_one = contract_cols(grad_proj_low, again[0])
    grad_in_norm, grad_gone, grad_sone = norm_one_back(grad_norm_one)
    input_grad = grad_middle + grad_in_norm
    owned_sums = (
        lax.psum_scatter(
            grad_wqkv.astype(jnp.bfloat16), "shard", scatter_dimension=0, tiled=True
        ).astype(jnp.float32),
        lax.psum_scatter(
            grad_bqv.astype(jnp.bfloat16), "shard", scatter_dimension=0, tiled=True
        ).astype(jnp.float32),
        lax.psum_scatter(
            grad_wout.astype(jnp.bfloat16), "shard", scatter_dimension=0, tiled=True
        ).astype(jnp.float32),
        lax.psum_scatter(
            grad_bout.astype(jnp.bfloat16), "shard", scatter_dimension=0, tiled=True
        ).astype(jnp.float32),
        lax.psum_scatter(
            grad_wup.astype(jnp.bfloat16), "shard", scatter_dimension=0, tiled=True
        ).astype(jnp.float32),
        lax.psum_scatter(
            grad_bup.astype(jnp.bfloat16), "shard", scatter_dimension=0, tiled=True
        ).astype(jnp.float32),
        lax.psum_scatter(
            grad_wdown.astype(jnp.bfloat16), "shard", scatter_dimension=0, tiled=True
        ).astype(jnp.float32),
        lax.psum_scatter(
            grad_bdown.astype(jnp.bfloat16), "shard", scatter_dimension=0, tiled=True
        ).astype(jnp.float32),
        lax.psum_scatter(
            grad_gone.astype(jnp.bfloat16), "shard", scatter_dimension=0, tiled=True
        ).astype(jnp.float32),
        lax.psum_scatter(
            grad_sone.astype(jnp.bfloat16), "shard", scatter_dimension=0, tiled=True
        ).astype(jnp.float32),
        lax.psum_scatter(
            grad_gtwo.astype(jnp.bfloat16), "shard", scatter_dimension=0, tiled=True
        ).astype(jnp.float32),
        lax.psum_scatter(
            grad_stwo.astype(jnp.bfloat16), "shard", scatter_dimension=0, tiled=True
        ).astype(jnp.float32),
    )
    totals = lax.psum(
        (
            owned_sums[0],
            owned_sums[1],
            owned_sums[2],
            owned_sums[3],
            owned_sums[4],
            owned_sums[5],
            owned_sums[6],
            owned_sums[7],
            owned_sums[8],
            owned_sums[9],
            owned_sums[10],
            owned_sums[11],
        ),
        "rep",
    )
    return (
        result,
        input_grad,
        totals[0],
        totals[1],
        totals[2],
        totals[3],
        totals[4],
        totals[5],
        totals[6],
        totals[7],
        totals[8],
        totals[9],
        totals[10],
        totals[11],
    )


def solution(mesh):
    return jax.shard_map(
        on_device,
        mesh=mesh,
        in_specs=(
            P(("rep", "shard"), None),
            P("shard", None),
            P("shard"),
            P("shard", None),
            P("shard"),
            P("shard", None),
            P("shard"),
            P("shard", None),
            P("shard"),
            P("shard"),
            P("shard"),
            P("shard"),
            P("shard"),
            P(("rep", "shard"), None),
        ),
        out_specs=(
            P(("rep", "shard"), None),
            P(("rep", "shard"), None),
            P("shard", None),
            P("shard"),
            P("shard", None),
            P("shard"),
            P("shard", None),
            P("shard"),
            P("shard", None),
            P("shard"),
            P("shard"),
            P("shard"),
            P("shard"),
            P("shard"),
        ),
        check_vma=False,
    )
```

profile of v0, /device:TPU:0, one launch (start us, length us, event | category | flops | bytes accessed | tf_op | source)
XLA Modules:
  0.0 907.6 jit_solution(9722744162934120144)
XLA Ops:
  9.5 5.8 all-gather
  15.4 5.8 all-gather.1
  21.3 5.8 all-gather.2
  27.6 38.0 %all-gather.13.cloned.1.call-done = bf16[768,2304]{1,0:T(8,128)(2,1)} async-done(((bf16[384,2304]{1,0:T(8,128)(2,1)}), bf16[768,2304]{1,0:T(8,128)(2,1)}) %all-gather.13.cloned.1.call-update) | async-done | bytes 3538960 | tf_op jit(solution)/shard_map/all_gather | solution.py:54
  65.6 3.2 fusion.78
  70.0 3.2 collective-permute-start
  73.3 28.8 %all-gather.3 = bf16[2,1,384]{2,1,0:T(2,128)(2,1)S(1)} all-gather(bf16[1,1,384]{2,1,0:T(2,128)(2,1)S(1)} %reshape.169), channel_id=1, replica_groups=mesh['rep'=64,'shard'=2] {'shard'}, dimensions={0}, use_global_device_ids=true | all-gather | bytes 2304 | tf_op jit(solution)/shard_map/all_gather | solution.py:57
  102.7 6.0 all-gather.4
  108.8 5.8 all-gather.5
  114.7 5.9 all-gather.6
  126.7 2.4 copy.48
  130.3 1.8 copy.47
  132.8 45.9 %while.28 = (s32[]{:T(128)}, bf16[12,256,64]{1,2,0:T(8,128)(2,1)}, f32[12,256,1]{1,2,0:T(1,128)}, bf16[12,256,64]{2,1,0:T(8,128)(2,1)}, bf16[12,512,64]{2,1,0:T(...) while((s32[]{:T(128)}, bf16[12,256,64]{1,2,0:T(8,128)(2,1)}, ...), condition=%wide.region_5.6_spmd.clone, body=%wide.region_2.5_spmd.clone.sunk | while | flops 34733824 | bytes 1982065 | solution.py:107
  134.2 1.8 fusion.129
  138.1 1.8 fusion.129
  141.9 1.8 fusion.129
  145.7 1.8 fusion.129
  149.6 1.8 fusion.129
  153.4 1.8 fusion.129
  157.2 1.8 fusion.129
  161.0 1.8 fusion.129
  164.8 1.8 fusion.129
  168.6 1.8 fusion.129
  172.4 1.8 fusion.129
  176.3 1.8 fusion.129
  179.9 2.0 fusion.90
  182.2 6.1 fusion.91
  188.2 52.8 %all-gather.17.cloned.1.call-done = bf16[768,3072]{1,0:T(8,128)(2,1)} async-done(((bf16[384,3072]{1,0:T(8,128)(2,1)}), bf16[768,3072]{1,0:T(8,128)(2,1)}) %all-gather.17.cloned.1.call-update) | async-done | bytes 4718608 | tf_op jit(solution)/shard_map/all_gather | solution.py:58
  241.0 8.6 fusion.82
  249.7 2.1 multiply_reduce_fusion.1
  256.0 2.6 convolution_convert_fusion.4
  258.6 1.9 copy.49
  261.6 91.8 %while.29 = (s32[]{:T(128)}, bf16[12,256,64]{1,2,0:T(8,128)(2,1)}, f32[12,512,64]{1,2,0:T(8,128)}, f32[12,512,64]{1,2,0:T(8,128)S(1)}, bf16[12,256,64]{2,1,0:T(8...) while((s32[]{:T(128)}, bf16[12,256,64]{1,2,0:T(8,128)(2,1)}, ...), condition=%wide.region_12.13_spmd.clone, body=%wide.region_10.12_spmd.clone.sunk | while | flops 85196544 | bytes 4863625 | solution.py:172
  264.9 1.7 fusion.139
  267.6 1.7 fusion.140
  272.5 1.7 fusion.139
  275.2 1.7 fusion.140
  280.2 1.7 fusion.139
  282.8 1.7 fusion.140
  287.8 1.7 fusion.139
  295.5 1.7 fusion.139
  298.2 1.7 fusion.140
  303.1 1.7 fusion.139
  305.8 1.7 fusion.140
  310.7 1.7 fusion.139
  318.4 1.7 fusion.139
  326.0 1.7 fusion.139
  333.7 1.7 fusion.139
  341.3 1.7 fusion.139
  349.0 1.7 fusion.139
  353.4 1.8 fusion.52
  356.6 21.3 %collective-permute-done.1 = bf16[256,1536]{0,1:T(8,128)(2,1)S(1)} collective-permute-done((bf16[256,1536]{0,1:T(8,128)(2,1)S(1)}, bf16[256,1536]{0,1:T(8,128)(2,1)S(1)}, u32[]{:S(2)}, u32[]{:S(2)}) %collective-permute-start.1) | collective-permute-done | bytes 786464 | tf_op jit(solution)/shard_map/ppermute | solution.py:15
  379.3 3.1 convolution_convert_fusion.2
  383.4 6.3 convolution_convert_fusion
  390.5 5.5 convolution_convert_fusion.1
  399.2 5.8 all-gather.7
  405.1 6.1 fusion.55
  411.7 1.8 fusion.81
  413.9 9.4 %all-reduce.9 = (bf16[1536]{0:T(1024)(128)(2,1)S(1)}, bf16[768]{0:T(1024)(128)(2,1)S(1)}, bf16[3072]{0:T(1024)(128)(2,1)S(1)}, bf16[768]{0:T(1024)(128)(2,1)S(1)...) all-reduce(bf16[1536]{0:T(1024)(128)(2,1)S(1)} %pad_maximum_fusion., ...), channel_id=3, replica_groups=mesh['rep'=64,'shard'=2] {'shard'}, use_global_device_ids=true, to_apply=%region_18.19.clone | all-reduce | flops 9216 | bytes 36864
  423.7 1.9 add_add_fusion.2
  425.7 8.2 reduce-scatter.5.cloned.1.call-done
  433.8 66.5 %reduce-scatter.11.cloned.1.call-done = bf16[1536,768]{1,0:T(8,128)(2,1)} async-done(((bf16[3072,768]{1,0:T(8,128)(2,1)}), bf16[1536,768]{1,0:T(8,128)(2,1)}) %reduce-scatter.11.cloned.1.call-update) | async-done | bytes 2359312 | tf_op jit(solution)/shard_map/reduce_scatter | solution.py:209
  500.3 66.6 %reduce-scatter.9.cloned.1.call-done = bf16[384,3072]{1,0:T(8,128)(2,1)} async-done(((bf16[768,3072]{1,0:T(8,128)(2,1)}), bf16[384,3072]{1,0:T(8,128)(2,1)}) %reduce-scatter.9.cloned.1.call-update) | async-done | bytes 2359312 | tf_op jit(solution)/shard_map/reduce_scatter | solution.py:203
  566.9 333.8 %all-reduce.11 = (f32[384,2304]{1,0:T(8,128)}, f32[768]{0:T(1024)}, f32[384,768]{1,0:T(8,128)}, f32[384]{0:T(512)}, f32[384,3072]{1,0:T(8,128)}, /*index=5*/f32[...) all-reduce(bf16[384,2304]{1,0:T(8,128)(2,1)} %reduce-scatter.5.clon, ...), channel_id=1, replica_groups=mesh['rep'=64,'shard'=2] {'rep'}, use_global_device_ids=true, to_apply=%region_16.17 | all-reduce | flops 3543552 | bytes 21270528 | tf_op jit(solution)/shard_map/psum | solution.py:228
  (278 shorter events, 112.2 us)
Async XLA Ops:
  7.2 2.3 copy-start.29
  7.2 8.2 copy-start.30
  7.2 14.1 %copy-start.28 = (bf16[768]{0:T(1024)(128)(2,1)S(1)}, bf16[768]{0:T(1024)(128)(2,1)}, u32[]{:S(2)}) copy-start(bf16[768]{0:T(1024)(128)(2,1)} %param.20) | copy-start | bytes 4612
  7.2 20.0 %copy-start = (bf16[256,768]{1,0:T(8,128)(2,1)S(1)}, bf16[256,768]{1,0:T(8,128)(2,1)}, u32[]{:S(2)}) copy-start(bf16[256,768]{1,0:T(8,128)(2,1)} %param.18) | copy-start | bytes 1179652
  7.2 58.4 %all-gather.13.cloned.1.call-start = ((), (), s32[]{:S(2)}) async-start(), calls=%async_computation.4 | async-start | bytes 5308416 | tf_op jit(solution)/shard_map/all_gather | solution.py:54
  8.0 170.8 %all-gather.15.cloned.1.call-start = ((), (), s32[]{:S(2)}) async-start(), calls=%async_computation.5 | async-start | bytes 1769472 | tf_op jit(solution)/shard_map/all_gather | solution.py:56
  8.7 173.5 %all-gather.19.cloned.1.call-start = ((), (), s32[]{:S(2)}) async-start(), calls=%async_computation.7 | async-start | bytes 7077888 | tf_op jit(solution)/shard_map/all_gather | solution.py:60
  9.4 231.6 %all-gather.17.cloned.1.call-start = ((), (), s32[]{:S(2)}) async-start(), calls=%async_computation.6 | async-start | bytes 7077888 | tf_op jit(solution)/shard_map/all_gather | solution.py:58
  27.3 41.5 %copy-start.13 = (f32[256]{0:T(256)}, f32[256]{0:T(256)S(1)}, u32[]{:S(2)}) copy-start(f32[256]{0:T(256)S(1)} %broadcast_multiply_fusion.1) | copy-start | bytes 3076
  27.6 41.2 %copy-start.24 = (f32[256]{0:T(256)}, f32[256]{0:T(256)S(1)}, u32[]{:S(2)}) copy-start(f32[256]{0:T(256)S(1)} %fusion.65) | copy-start | bytes 3076
  27.6 41.2 %copy-start.16 = (f32[256]{0:T(256)}, f32[256]{0:T(256)S(1)}, u32[]{:S(2)}) copy-start(f32[256]{0:T(256)S(1)} %fusion.73) | copy-start | bytes 3076
  68.9 4.4 copy-start.31
  68.9 33.8 %copy-start.32 = (bf16[384]{0:T(512)(128)(2,1)S(1)}, bf16[384]{0:T(512)(128)(2,1)}, u32[]{:S(2)}) copy-start(bf16[384]{0:T(512)(128)(2,1)} %param.29) | copy-start | bytes 2308
  68.9 39.8 %copy-start.33 = (bf16[384]{0:T(512)(128)(2,1)S(1)}, bf16[384]{0:T(512)(128)(2,1)}, u32[]{:S(2)}) copy-start(bf16[384]{0:T(512)(128)(2,1)} %param.30) | copy-start | bytes 2308
  68.9 45.7 %copy-start.27 = (bf16[1536]{0:T(1024)(128)(2,1)S(1)}, bf16[1536]{0:T(1024)(128)(2,1)}, u32[]{:S(2)}) copy-start(bf16[1536]{0:T(1024)(128)(2,1)} %param.24) | copy-start | bytes 9220
  70.0 54.2 %collective-permute-start = (bf16[256,1536]{1,0:T(8,128)(2,1)}, bf16[256,1536]{1,0:T(8,128)(2,1)}, u32[]{:S(2)}, u32[]{:S(2)}) collective-permute-start(bf16[256,1536]{1,0:T(8,128)(2,1)} %pad_maximum_fusion.2), channel_id=1, source_target_pairs={{0,1},{2,3},{4,5},{6,7},{8,9},{10,11},{12,13},{14,15},{16,17},{18,... | collective-permute-start | bytes 2359304 | tf_op jit(solution)/shard_map/ppermute | solution.py:15
  73.2 352.5 %reduce-scatter.7.cloned.1.call-start = ((), (), s32[]{:S(2)}) async-start(), calls=%async_computation.9 | async-start | bytes 1769472 | tf_op jit(solution)/shard_map/reduce_scatter | solution.py:197
  178.7 1.2 copy-start.3
  179.9 2.3 copy-start.4
  181.9 67.8 %copy-start.19 = (f32[256]{0:T(256)}, f32[256]{0:T(256)S(1)}, u32[]{:S(2)}) copy-start(f32[256]{0:T(256)S(1)} %broadcast_multiply_fusion) | copy-start | bytes 3076
  182.1 67.6 %copy-start.21 = (f32[256]{0:T(256)}, f32[256]{0:T(256)S(1)}, u32[]{:S(2)}) copy-start(f32[256]{0:T(256)S(1)} %fusion.74) | copy-start | bytes 3076
  182.1 58.9 %copy-start.23 = (f32[2,1,1536]{2,1,0:T(1,128)S(1)}, f32[2,1,1536]{2,1,0:T(1,128)}, u32[]{:S(2)}) copy-start(f32[2,1,1536]{2,1,0:T(1,128)} %convert_element_type.210) | copy-start | bytes 36868
  241.0 8.7 copy-start.35
  249.7 2.1 copy-start.12
  249.7 3.2 copy-start.5
  251.8 2.7 copy-start.9
  252.9 0.9 copy-start.26
  253.8 0.7 copy-start.10
  260.6 173.2 %reduce-scatter.5.cloned.1.call-start = ((), (), s32[]{:S(2)}) async-start(), calls=%async_computation.8 | async-start | bytes 5308416 | tf_op jit(solution)/shard_map/reduce_scatter | solution.py:191
  353.4 3.2 copy-start.1
  353.4 3.2 copy-start.11
  353.4 24.5 %copy-start.2 = (f32[12,512,64]{1,2,0:T(8,128)S(1)}, f32[12,512,64]{1,2,0:T(8,128)}, u32[]{:S(2)}) copy-start(f32[12,512,64]{1,2,0:T(8,128)} %get-tuple-element.109) | copy-start | bytes 4718596
  355.2 24.1 %copy-start.14 = (f32[256]{0:T(256)S(1)}, f32[256]{0:T(256)}, u32[]{:S(2)}) copy-start(f32[256]{0:T(256)} %copy-done.13) | copy-start | bytes 3076
  355.2 24.1 %copy-start.17 = (f32[256]{0:T(256)S(1)}, f32[256]{0:T(256)}, u32[]{:S(2)}) copy-start(f32[256]{0:T(256)} %copy-done.16) | copy-start | bytes 3076
  355.2 22.7 %collective-permute-start.1 = (bf16[256,1536]{0,1:T(8,128)(2,1)S(1)}, bf16[256,1536]{0,1:T(8,128)(2,1)S(1)}, u32[]{:S(2)}, u32[]{:S(2)}) collective-permute-start(bf16[256,1536]{0,1:T(8,128)(2,1)S(1)} %fusion.52), channel_id=1, source_target_pairs={{1,0},{3,2},{5,4},{7,6},{9,8},{11,10},{13,12},{15,14},{17,16},{19,... | collective-permute-start | bytes 2359304 | tf_op jit(solution)/shard_map/ppermute | solution.py:15
  356.6 22.7 %copy-start.7 = (bf16[12,256,64]{1,2,0:T(8,128)(2,1)}, bf16[12,256,64]{1,2,0:T(8,128)(2,1)S(1)}, u32[]{:S(2)}) copy-start(bf16[12,256,64]{1,2,0:T(8,128)(2,1)S(1)} %convert_multiply_fusion) | copy-start | bytes 1179652
  382.4 1.0 copy-start.6
  382.5 117.8 %reduce-scatter.11.cloned.1.call-start = ((), (), s32[]{:S(2)}) async-start(), calls=%async_computation.11 | async-start | bytes 7077888 | tf_op jit(solution)/shard_map/reduce_scatter | solution.py:209
  389.8 0.7 copy-start.20
  389.8 0.7 copy-start.22
  389.8 177.1 %reduce-scatter.9.cloned.1.call-start = ((), (), s32[]{:S(2)}) async-start(), calls=%async_computation.10 | async-start | bytes 7077888 | tf_op jit(solution)/shard_map/reduce_scatter | solution.py:203
  396.0 0.7 copy-start.37
  396.0 3.2 copy-start.34
  405.0 6.2 copy-start.8
  405.0 6.6 copy-start.15
  405.1 6.6 copy-start.36
  411.6 1.8 copy-start.25
  411.6 1.8 copy-start.18
Sparse Core Ops, SparseCore 0:
  9.7 55.8 all-gather.12
  67.3 34.1 all-gather.14
  103.2 70.0 all-gather.18
  174.8 66.1 all-gather.16
  260.7 25.1 reduce-scatter.6
  382.6 51.1 reduce-scatter.4
  436.8 63.4 reduce-scatter.10
  503.4 63.4 reduce-scatter.8
where the time goes:
time: 911 us; the launch traced here: 908 us
  blocking collectives  413 us (45%)
  waiting for transfers between devices  255 us (28%)
  matrix products  167 us (18%)
  local copies, waits for them, and re-layouts  31.9 us (4%)
  other arithmetic  17.9 us (2%)
  between operations  16.7 us (2%)
    psum x1, blocking collectives, on_device(): lax.psum((owned_sums[0], owned_sums[1], owned_sums[2], owned_sums[3], own...  334 us
    reduce_scatter x1, waiting for transfers between devices, on_device(): lax.psum_scatter(grad_wup.astype(jnp.bfloat16), 'shard', scatter_dimensio...  66.6 us
    reduce_scatter x1, waiting for transfers between devices, on_device(): lax.psum_scatter(grad_wdown.astype(jnp.bfloat16), 'shard', scatter_dimens...  66.5 us
    all_gather x1, waiting for transfers between devices, on_device(): lax.all_gather(w_up, 'shard', axis=0, tiled=True)  52.8 us
    dot_general x28, matrix products, contract_rows(): lax.dot_general(left, right, (((0,), (0,)), ((), ())), preferred_element_...  48 us
    all_gather x1, waiting for transfers between devices, on_device(): lax.all_gather(w_qkv, 'shard', axis=0, tiled=True)  38 us
    dot_general x24, matrix products, score_block(): lax.dot_general(query_one, key_one, (((1,), (1,)), ((), ())), preferred_e...  29.8 us
    all_gather x1, blocking collectives, on_device(): lax.all_gather(b_out, 'shard', axis=0, tiled=True)  28.8 us
  transfers between devices with their start and end apart: 10, of which 6 were waited for; matrix products, arithmetic and copies ran while one was open for 21% of the time, Pallas kernels for 0%

commit v1 on v0

v1 whole, which is shorter than its diff:
```python
import functools
import jax
import jax.numpy as jnp
from jax import lax
from jax.experimental import pallas as pl
from jax.experimental.pallas import tpu as pltpu
from jax.sharding import Mesh
from jax.sharding import PartitionSpec as P

HEAD_DIM = 64
eps = 1e-05
F32 = jnp.float32
BF16 = jnp.bfloat16
VMEM_LIMIT = 56 * 1024 * 1024


def dot_nn(left, right):
    return lax.dot_general(left, right, (((1,), (0,)), ((), ())), preferred_element_type=F32)


def dot_nt(left, right):
    return lax.dot_general(left, right, (((1,), (1,)), ((), ())), preferred_element_type=F32)


def dot_tn(left, right):
    return lax.dot_general(left, right, (((0,), (0,)), ((), ())), preferred_element_type=F32)


def normalise(values):
    center = jnp.mean(values, axis=-1, keepdims=True)
    centered = values - center
    spread = jnp.mean(centered * centered, axis=-1, keepdims=True)
    scale = lax.rsqrt(spread + eps)
    return centered * scale, scale


def norm_back(unit, scale, upstream, gain):
    q = upstream * gain
    return scale * (
        q
        - jnp.mean(q, axis=-1, keepdims=True)
        - unit * jnp.mean(q * unit, axis=-1, keepdims=True)
    )


def column_sum(values):
    return jnp.sum(values, axis=0, keepdims=True)


def two_heads(block):
    lane = lax.broadcasted_iota(jnp.int32, block.shape, 1)
    zero = jnp.zeros_like(block)
    return jnp.concatenate(
        [jnp.where(lane < HEAD_DIM, block, zero), jnp.where(lane < HEAD_DIM, zero, block)], axis=0
    )


def merge_heads(rows_t, count):
    row = lax.broadcasted_iota(jnp.int32, (2 * HEAD_DIM, count), 0)
    return jnp.transpose(
        jnp.where(row < HEAD_DIM, rows_t[:, :count], rows_t[:, count:]), (1, 0)
    )


def masked_scores(keys_two, queries_two, hidden_prev, count):
    scores = dot_nt(keys_two, queries_two)
    key = lax.broadcasted_iota(jnp.int32, (count, 2 * count), 0)
    query = lax.broadcasted_iota(jnp.int32, (count, 2 * count), 1)
    query = jnp.where(query >= count, query - count, query)
    prev = scores[:count] + hidden_prev
    here = jnp.where(key <= query, scores[count:], -1e30)
    return jnp.concatenate([prev, here], axis=0)


def assemble(place, parts, target, sems, first):
    own, near, far = parts
    half, quarter = own.shape[0], near.shape[0]
    shard, core = place[0], place[1]
    starts = (
        shard * half,
        (1 - shard) * half + core * quarter,
        (1 - shard) * half + (1 - core) * quarter,
    )
    copies = []
    for index, (part, start) in enumerate(zip(parts, starts)):
        rows = pl.ds(pl.multiple_of(start, quarter), part.shape[0])
        copies.append(pltpu.make_async_copy(part, target.at[rows], sems.at[first + index]))
        copies[-1].start()
    return copies


def finish(copies):
    for copy in copies:
        copy.wait()


def store_columns(target, core, chunk, value):
    blocks, wide = target.shape[3], target.shape[5]
    value = value.astype(BF16)
    for half in range(value.shape[1] // wide):
        place = chunk * (value.shape[1] // wide) + half
        block = value[:, half * wide : (half + 1) * wide].reshape(
            target.shape[1], target.shape[2], target.shape[4], wide
        )
        target[lax.rem(core + place // blocks, 2), :, :, place % blocks] = block


def forward_attention(
    place, x_prev, x_here, own, near, far, b_qv, gain, shift,
    normed, queries, keys, values, attended, log_total, w_qkv, sems,
):
    copies = assemble(place, (own, near, far), w_qkv, sems, 0)
    rows, width = x_here.shape
    hidden_prev = jnp.where(place[0] > 0, 0.0, -1e30).astype(F32)
    for part, source in enumerate((x_prev, x_here)):
        unit, _ = normalise(source[...].astype(F32))
        normed[part * rows : (part + 1) * rows, :] = (unit * gain[...] + shift[...]).astype(BF16)
    finish(copies)
    here = normed[rows:, :]
    queries[...] = ((dot_nn(here, w_qkv[:, :width]) + b_qv[:, :width]) * 0.125).astype(BF16)
    keys[...] = dot_nn(normed[...], w_qkv[:, width : 2 * width]).astype(BF16)
    values[...] = (dot_nn(normed[...], w_qkv[:, 2 * width :]) + b_qv[:, width:]).astype(BF16)
    for pair in range(width // (2 * HEAD_DIM)):
        at = slice(pair * 2 * HEAD_DIM, (pair + 1) * 2 * HEAD_DIM)
        scores = masked_scores(keys[:, at], two_heads(queries[:, at]), hidden_prev, rows)
        top = jnp.max(scores, axis=0, keepdims=True)
        expo = jnp.exp(scores - top)
        total = jnp.sum(expo, axis=0, keepdims=True)
        probs_low = (expo * (1.0 / total)).astype(BF16)
        log_total[pair : pair + 1, :] = top + jnp.log(total)
        attended[:, at] = merge_heads(dot_tn(values[:, at], probs_low), rows).astype(BF16)


def forward_middle(
    place, attended, x_here, out_own, out_near, out_far, b_out, gain, shift,
    up_own, up_near, up_far, b_up, cotangent,
    middle, normed, hidden, activated, grad_w_down, grad_b_down, w_out, w_up, sems,
):
    out_copies = assemble(place, (out_own, out_near, out_far), w_out, sems, 0)
    up_copies = assemble(place, (up_own, up_near, up_far), w_up, sems, 3)
    finish(out_copies)
    rows, width = x_here.shape
    mid = x_here[...].astype(F32) + (dot_nn(attended[...], w_out[...]) + b_out[...])
    middle[...] = mid
    unit, _ = normalise(mid)
    normed[...] = (unit * gain[...] + shift[...]).astype(BF16)
    finish(up_copies)
    for chunk in range(w_up.shape[1] // width):
        at = slice(chunk * width, (chunk + 1) * width)
        hid = dot_nn(normed[...], w_up[:, at]) + b_up[:, at]
        hidden[:, at] = hid
        low = jax.nn.gelu(hid, approximate=True).astype(BF16)
        activated[:, at] = low
        part = dot_tn(low, cotangent[...]).astype(BF16)
        grad_w_down[lax.rem(place[1] + chunk, 2), chunk // 2] = part
    grad_b_down[...] = column_sum(cotangent[...].astype(F32))


def gelu_slope(u):
    c = 0.7978845608028654
    t = jnp.tanh(c * (u + 0.044715 * (u * u * u)))
    return 0.5 * (1.0 + t) + 0.5 * u * (1.0 - t * t) * (c * (1.0 + 3.0 * 0.044715 * (u * u)))


def middle_back(
    place, cotangent, hidden, activated, normed, middle, own, near, far, b_down,
    result, grad_hidden, grad_w_up, grad_b_up, w_down, sems,
):
    finish(assemble(place, (own, near, far), w_down, sems, 0))
    rows, width = middle.shape
    ct = cotangent[...]
    out = jnp.zeros((rows, width), F32)
    for chunk in range(w_down.shape[0] // width):
        at = slice(chunk * width, (chunk + 1) * width)
        grad_act = dot_nt(ct, w_down[at, :])
        grad_hid = (grad_act * gelu_slope(hidden[:, at])).astype(BF16)
        grad_hidden[:, at] = grad_hid
        grad_b_up[:, at] = column_sum(grad_hid.astype(F32))
        store_columns(grad_w_up, place[1], chunk, dot_tn(normed[...], grad_hid))
        out = out + dot_nn(activated[:, at], w_down[at, :])
    result[...] = (middle[...] + (out + b_down[...])).astype(result.dtype)


def input_back(
    place, x_prev, x_here, cotangent, middle, grad_hidden, gain_two, attended,
    normed, queries, keys, values, log_total, gain_one,
    up_own, up_near, up_far, out_own, out_near, out_far, qkv_own, qkv_near, qkv_far,
    input_grad, prev_grad, grad_w_attn, small,
    grad_att, grad_proj, w_up, w_out, w_qkv, sems,
):
    up_copies = assemble(place, (up_own, up_near, up_far), w_up, sems, 0)
    out_copies = assemble(place, (out_own, out_near, out_far), w_out, sems, 3)
    qkv_copies = assemble(place, (qkv_own, qkv_near, qkv_far), w_qkv, sems, 6)
    finish(up_copies)
    finish(out_copies)
    finish(qkv_copies)
    rows, width = x_here.shape
    hidden_prev = jnp.where(place[0] > 0, 0.0, -1e30).astype(F32)
    grad_norm = dot_nt(grad_hidden[...], w_up[...])
    unit, scale = normalise(middle[...])
    small[4:5, :] = column_sum(grad_norm * unit)
    small[5:6, :] = column_sum(grad_norm)
    grad_mid = cotangent[...].astype(F32) + norm_back(unit, scale, grad_norm, gain_two[...])
    grad_branch = grad_mid.astype(BF16)
    input_grad[...] = grad_mid
    small[6:7, :] = column_sum(grad_branch.astype(F32))
    grad_att[...] = dot_nt(grad_branch, w_out[...]).astype(BF16)
    store_columns(grad_w_attn, place[1], 3, dot_tn(attended[...], grad_branch))
    grad_proj[:rows, :width] = jnp.zeros((rows, width), BF16)
    for pair in range(width // (2 * HEAD_DIM)):
        at = slice(pair * 2 * HEAD_DIM, (pair + 1) * 2 * HEAD_DIM)
        queries_two = two_heads(queries[:, at])
        grads_two = two_heads(grad_att[:, at])
        scores = masked_scores(keys[:, at], queries_two, hidden_prev, rows)
        probs = jnp.exp(scores - log_total[pair : pair + 1, :])
        probs_low = probs.astype(BF16)
        grad_probs = dot_nt(values[:, at], grads_two)
        inner = jnp.sum(probs * grad_probs, axis=0, keepdims=True)
        grad_scores = (probs * (grad_probs - inner)).astype(BF16)
        first, last = pair * 2 * HEAD_DIM, (pair + 1) * 2 * HEAD_DIM
        grad_queries = merge_heads(dot_tn(keys[:, at], grad_scores), rows)
        grad_proj[rows:, at] = (grad_queries.astype(BF16) * 0.125).astype(BF16)
        grad_proj[:, width + first : width + last] = dot_nn(grad_scores, queries_two).astype(BF16)
        grad_proj[:, 2 * width + first : 2 * width + last] = dot_nn(probs_low, grads_two).astype(BF16)
    for chunk in range(3):
        at = slice(chunk * width, (chunk + 1) * width)
        store_columns(grad_w_attn, place[1], chunk, dot_tn(normed[...], grad_proj[:, at]))
    small[0:1, :] = column_sum(grad_proj[:, :width].astype(F32))
    small[1:2, :] = column_sum(grad_proj[:, 2 * width :].astype(F32))
    gain_sum = jnp.zeros((1, width), F32)
    shift_sum = jnp.zeros((1, width), F32)
    for part, source in enumerate((x_prev, x_here)):
        at = slice(part * rows, (part + 1) * rows)
        first = (1 - part) * width
        grad_norm = dot_nt(grad_proj[at, first:], w_qkv[:, first:])
        unit, scale = normalise(source[...].astype(F32))
        gain_sum = gain_sum + column_sum(grad_norm * unit)
        shift_sum = shift_sum + column_sum(grad_norm)
        grad_in = norm_back(unit, scale, grad_norm, gain_one[...])
        if part == 0:
            prev_grad[...] = grad_in.astype(prev_grad.dtype)
        else:
            input_grad[...] = input_grad[...] + grad_in
    small[2:3, :] = gain_sum
    small[3:4, :] = shift_sum
    small[7:8, :] = jnp.zeros((1, width), F32)


VM = pl.BlockSpec(memory_space=pltpu.VMEM)
SM = pl.BlockSpec(memory_space=pltpu.SMEM)


def call(body, outs, flops, moved, in_specs, scratch=()):
    return pl.pallas_call(
        body,
        out_shape=tuple(jax.ShapeDtypeStruct(s, d) for s, d in outs),
        in_specs=in_specs,
        out_specs=tuple(VM for _ in outs),
        scratch_shapes=list(scratch),
        compiler_params=pltpu.CompilerParams(vmem_limit_bytes=VMEM_LIMIT),
        cost_estimate=pl.CostEstimate(flops=flops, bytes_accessed=moved, transcendentals=0),
    )


CHIPS = ("y_hi", "x", "z", "y_lo")
COPIES = ("x", "z", "y_lo")
SWAP = [(0, 1), (1, 0)]
ACROSS = [(0, 3), (1, 2), (2, 1), (3, 0)]


def fetch(shard, core):
    quarter = shard.shape[0] // 2
    mine = lax.dynamic_slice_in_dim(shard, core * quarter, quarter, 0)
    near = lax.ppermute(mine, ("y_lo", "y_hi"), ACROSS)
    far = lax.ppermute(near, "core", SWAP)
    return shard, near, far


def reduce_chunks(chunks):
    other = lax.ppermute(chunks[1], "core", SWAP)
    both = (chunks[0].astype(F32) + other.astype(F32)).astype(BF16)
    spread = lax.all_to_all(both, CHIPS, 0, 0, tiled=True)
    return jnp.sum(spread, axis=0, dtype=F32).astype(BF16)


def gather_chunks(chunk):
    copies = 1
    for axis in COPIES:
        copies *= lax.axis_size(axis)
    mine = lax.all_to_all(
        jnp.broadcast_to(chunk[None], (copies,) + chunk.shape), COPIES, 0, 0, tiled=True
    )
    return mine, lax.ppermute(mine, "core", SWAP)


def ordered(core, mine, other):
    first = jnp.where(core == 0, mine, other)
    last = jnp.where(core == 0, other, mine)
    return jnp.stack([first, last]).astype(F32)


def on_device(
    tokens, w_qkv, b_qv, w_out, b_out, w_up, b_up, w_down, b_down,
    gain_one, shift_one, gain_two, shift_two, cotangent,
):
    rows, width = tokens.shape
    ff = w_up.shape[1]
    shard = lax.axis_index("y_hi")
    core = lax.axis_index("core")
    place = jnp.stack([shard, core]).astype(jnp.int32)
    x_prev = lax.ppermute(tokens, "y_hi", [(0, 1)])
    vectors = (b_qv, b_out, b_down, gain_one, shift_one, gain_two, shift_two, b_up)
    packed = jnp.concatenate(vectors)
    got = lax.ppermute(packed, "y_hi", SWAP)
    low = jnp.where(shard == 0, packed, got).astype(F32)
    high = jnp.where(shard == 0, got, packed).astype(F32)
    whole, at = [], 0
    for vector in vectors:
        size = vector.shape[0]
        whole.append(jnp.concatenate([low[at : at + size], high[at : at + size]])[None])
        at += size
    c_qv, c_out, c_down, g_one, s_one, g_two, s_two, c_up = whole
    qkv = fetch(w_qkv, core)
    out = fetch(w_out, core)
    up = fetch(w_up, core)
    down = fetch(w_down, core)
    ANY = pl.BlockSpec(memory_space=pl.ANY)
    dma = pltpu.SemaphoreType.DMA
    pairs = width // (2 * HEAD_DIM)

    normed, queries, keys, values, attended, log_total = call(
        forward_attention,
        [((2 * rows, width), BF16), ((rows, width), BF16), ((2 * rows, width), BF16),
         ((2 * rows, width), BF16), ((rows, width), BF16), ((pairs, 2 * rows), F32)],
        12 * 10**9, 8 * 10**6,
        [SM, VM, VM, ANY, ANY, ANY, VM, VM, VM],
        [pltpu.VMEM((width, 3 * width), BF16), dma((3,))],
    )(place, x_prev, tokens, *qkv, c_qv, g_one, s_one)

    middle, normed_two, hidden, activated, grad_wd, grad_bd = call(
        forward_middle,
        [((rows, width), F32), ((rows, width), BF16), ((rows, ff), F32), ((rows, ff), BF16),
         ((2, 2, ff // 4, width), BF16), ((1, width), F32)],
        12 * 10**9, 16 * 10**6,
        [SM, VM, VM, ANY, ANY, ANY, VM, VM, VM, ANY, ANY, ANY, VM, VM],
        [pltpu.VMEM((width, width), BF16), pltpu.VMEM((width, ff), BF16), dma((6,))],
    )(place, attended, tokens, *out, c_out, g_two, s_two, *up, c_up, cotangent)

    chips = 1
    for axis in CHIPS:
        chips *= lax.axis_size(axis)
    copies = chips // 2
    wide, tall = width // 2, width // 2 // (copies // 4)
    down_sum = reduce_chunks(grad_wd.reshape(2, chips, ff // 4 // copies, width))
    up_shape = (2, 2, copies // 4, 4, tall, wide)

    result, grad_hidden, grad_wu, grad_bu = call(
        middle_back,
        [((rows, width), BF16), ((rows, ff), BF16), (up_shape, BF16), ((1, ff), F32)],
        12 * 10**9, 16 * 10**6,
        [SM, VM, VM, VM, VM, VM, ANY, ANY, ANY, VM],
        [pltpu.VMEM((ff, width), BF16), dma((3,))],
    )(place, cotangent, hidden, activated, normed_two, middle, *down, c_down)
    up_sum = reduce_chunks(grad_wu.reshape(2, chips, tall, wide))

    input_grad, prev_grad, grad_wa, small = call(
        input_back,
        [((rows, width), F32), ((rows, width), BF16), (up_shape, BF16), ((8, width), F32)],
        20 * 10**9, 20 * 10**6,
        [SM] + [VM] * 13 + [ANY] * 9,
        [pltpu.VMEM((rows, width), BF16), pltpu.VMEM((2 * rows, 3 * width), BF16),
         pltpu.VMEM((width, ff), BF16), pltpu.VMEM((width, width), BF16),
         pltpu.VMEM((width, 3 * width), BF16), dma((9,))],
    )(place, x_prev, tokens, cotangent, middle, grad_hidden, g_two, attended, normed, queries,
      keys, values, log_total, g_one, *up, *out, *qkv)
    attn_sum = reduce_chunks(grad_wa.reshape(2, chips, tall, wide))
    input_grad = input_grad + lax.ppermute(prev_grad, "y_hi", [(1, 0)]).astype(F32)

    small = jnp.concatenate([small[:7], grad_bd, grad_bu.reshape(ff // width, width)], axis=0)
    small = lax.psum(small, CHIPS + ("core",))

    total_wd = ordered(core, *gather_chunks(down_sum)).reshape(ff // 2, width)

    def columns(chunk):
        both = ordered(core, *gather_chunks(chunk)).reshape(2, copies // 4, 4, tall, wide)
        return jnp.transpose(both, (1, 3, 0, 2, 4)).reshape(width // 2, ff)

    total_wu = columns(up_sum)
    total_wa = columns(attn_sum)

    def mine(vector):
        size = vector.shape[0] // 2
        return lax.dynamic_slice_in_dim(vector, shard * size, size, 0)

    return (
        result,
        input_grad,
        total_wa[:, : 3 * width],
        mine(small[:2].reshape(-1)),
        total_wa[:, 3 * width :],
        mine(small[6]),
        total_wu,
        mine(small[8:].reshape(-1)),
        total_wd,
        mine(small[7]),
        mine(small[2]),
        mine(small[3]),
        mine(small[4]),
        mine(small[5]),
    )


def solution(mesh):
    axes = ("x", "z", "y_lo", "core", "y_hi")
    fine = Mesh(mesh.devices.reshape(4, 4, 2, 2, 2), axes)
    split = P(axes, None)
    matrix, vector = P("y_hi", None), P("y_hi")
    params = (matrix, vector, matrix, vector, matrix, vector, matrix, vector) + (vector,) * 4
    return jax.shard_map(
        on_device,
        mesh=fine,
        in_specs=(split,) + params + (split,),
        out_specs=(split, split) + params,
        check_vma=False,
    )
```

time: 911 us -> 473 us (0.52)
  blocking collectives: 413 us -> 73.8 us
  matrix products: 167 us -> 0 us
  waiting for transfers between devices: 255 us -> 178 us
  Pallas kernels: 0 us -> 52.6 us
  starting transfers between devices: 4.95 us -> 53.3 us
  local copies, waits for them, and re-layouts: 31.9 us -> 77.7 us
  between operations: 16.7 us -> 1.48 us
  other arithmetic: 17.9 us -> 29.9 us
    psum x1, blocking collectives: 334 us -> 73.8 us  [on_device(): small = lax.psum(small, CHIPS + ('core',))]
    dot_general x96 -> x0, matrix products: 167 us -> none  [the longest x28 48 us: contract_rows(): lax.dot_general(left, right, (((0,), (0,)), ((), ())), preferred_element_...]
    reduce_scatter x4 -> x0, waiting for transfers between devices: 141 us -> none  [the longest x1 66.6 us: on_device(): lax.psum_scatter(grad_wup.astype(jnp.bfloat16), 'shard', scatter_dimensio...]
    all_to_all x0 -> x6, waiting for transfers between devices: none -> 110 us  [the longest x3 78.2 us: reduce_chunks(): spread = lax.all_to_all(both, CHIPS, 0, 0, tiled=True)]
    all_gather x4 -> x0, waiting for transfers between devices: 90.8 us -> none  [the longest x1 52.8 us: on_device(): lax.all_gather(w_up, 'shard', axis=0, tiled=True)]
    all_gather x8 -> x0, blocking collectives: 69.8 us -> none  [the longest x1 28.8 us: on_device(): lax.all_gather(b_out, 'shard', axis=0, tiled=True)]
    pallas_call x0 -> x4, Pallas kernels: none -> 52.6 us  [the longest x1 20.5 us: on_device(): call(input_back, [((rows, width), F32), ((rows, width), BF16), (up_shape,...]
    ppermute x2 -> x17, waiting for transfers between devices: 21.3 us -> 67.3 us  [the longest x4 67.3 us: fetch(): near = lax.ppermute(mine, ('y_lo', 'y_hi'), ACROSS)]
  transfers between devices with their start and end apart: 10 -> 23, of which waited for: 6 -> 9; matrix products, arithmetic and copies ran while one was open for 21% -> 17% of each run, Pallas kernels for 0% -> 11%
where the time goes in v1:
time: 473 us; the launch traced here: 467 us
  waiting for transfers between devices  178 us (38%)
  local copies, waits for them, and re-layouts  77.7 us (16%)
  blocking collectives  73.8 us (16%)
  starting transfers between devices  53.3 us (11%)
  Pallas kernels  52.6 us (11%)
  other arithmetic  29.9 us (6%)
    all_to_all x3, waiting for transfers between devices, reduce_chunks(): spread = lax.all_to_all(both, CHIPS, 0, 0, tiled=True)  78.2 us
    psum x1, blocking collectives, on_device(): small = lax.psum(small, CHIPS + ('core',))  73.8 us
    ppermute x4, waiting for transfers between devices, fetch(): near = lax.ppermute(mine, ('y_lo', 'y_hi'), ACROSS)  67.3 us
    all_to_all x3, waiting for transfers between devices, gather_chunks(): lax.all_to_all(jnp.broadcast_to(chunk[None], (copies,) + chunk.shape), CO...  32.2 us
    all_to_all x3, starting transfers between devices, reduce_chunks(): spread = lax.all_to_all(both, CHIPS, 0, 0, tiled=True)  25.2 us
    reshape x4, local copies, waits for them, and re-layouts, columns(): return jnp.transpose(both, (1, 3, 0, 2, 4)).reshape(width // 2, ff)  20.7 us
    pallas_call x1, Pallas kernels, on_device(): call(input_back, [((rows, width), F32), ((rows, width), BF16), (up_shape,...  20.5 us
    unnamed x21, local copies, waits for them, and re-layouts  13.2 us
  transfers between devices with their start and end apart: 23, of which 9 were waited for; matrix products, arithmetic and copies ran while one was open for 17% of the time, Pallas kernels for 11%

profile of v1, /device:TPU:0, one launch (start us, length us, event | category | flops | bytes accessed | tf_op | source)
XLA Modules:
  0.0 466.6 jit_solution(7883396158241602587)
XLA Ops:
  0.7 1.5 dynamic-update-slice
  2.2 1.4 dynamic-update-slice.1
  3.6 1.4 dynamic-update-slice.2
  5.1 1.4 dynamic-update-slice.3
  6.5 1.4 dynamic-update-slice.4
  7.9 1.4 dynamic-update-slice.5
  9.4 1.4 dynamic-update-slice.6
  10.8 1.3 constant_dynamic-update-slice_fusion
  12.1 3.3 collective-permute-start.3
  15.4 1.2 constant_dynamic-slice_fusion.9
  16.6 1.1 collective-permute-start.1
  17.8 4.3 collective-permute-start
  22.1 1.3 constant_dynamic-slice_fusion.7
  23.6 3.3 collective-permute-start.4
  26.9 1.3 constant_dynamic-slice_fusion.6
  29.6 16.7 %collective-permute-done.1.near.qkv_near = bf16[192,2304]{1,0:T(8,128)(2,1)} collective-permute-done((bf16[192,2304]{1,0:T(8,128)(2,1)S(1)}, bf16[192,2304]{1,0:T(8,128)(2,1)}, u32[]{:S(2)}, u32[]{:S(2)}) %collective-permute-start.1) | collective-permute-done | bytes 884768 | tf_op jit(solution)/shard_map/ppermute | solution.py:274
  47.0 24.6 %collective-permute-done.6.up_near = bf16[192,3072]{1,0:T(8,128)(2,1)} collective-permute-done((bf16[192,3072]{1,0:T(8,128)(2,1)S(1)}, bf16[192,3072]{1,0:T(8,128)(2,1)}, u32[]{:S(2)}, u32[]{:S(2)}) %collective-permute-start.6) | collective-permute-done | bytes 1179680 | tf_op jit(solution)/shard_map/ppermute | solution.py:274
  75.7 2.2 collective-permute-done.4.out_near
  77.9 23.8 %collective-permute-done.8.near = bf16[768,768]{1,0:T(8,128)(2,1)} collective-permute-done((bf16[768,768]{1,0:T(8,128)(2,1)S(1)}, bf16[768,768]{1,0:T(8,128)(2,1)}, u32[]{:S(2)}, u32[]{:S(2)}) %collective-permute-start.8) | collective-permute-done | bytes 1179680 | tf_op jit(solution)/shard_map/ppermute | solution.py:274
  103.1 8.8 %shard_map.245 = (bf16[512,768]{1,0:T(8,128)(2,1)}, bf16[256,768]{1,0:T(8,128)(2,1)}, bf16[512,768]{1,0:T(8,128)(2,1)}, bf16[512,768]{1,0:T(8,128)(2,1)}, bf16[256,768]{1,0:T(8,128)(2,1)}, /*index=5*/f32[6,512]{1,0:T(8,128)}) custom-call(s32[2]{0:T(128)} %pad_add_fusion.place, bf16[256,768]{1,0:T(8,128)(2,1)} %collective-permute-done.x_prev, ...), custom_call_target="tpu_custom_call" | custom-call | flops 12000000000 | bytes 8000000 | tf_op jit(solution)/shard_map/pallas_call | solution.py:331
  113.0 10.9 %shard_map.246 = (f32[256,768]{1,0:T(8,128)}, bf16[256,768]{1,0:T(8,128)(2,1)}, f32[256,3072]{1,0:T(8,128)}, bf16[256,3072]{1,0:T(8,128)(2,1)}, bf16[2,2,768,768]{3,2,1,0:T(8,128)(2,1)}, /*index=5*/f32[1,768]{1,0:T(1,128)}) custom-call(s32[2]{0:T(128)} %pad_add_fusion.place, bf16[256,768]{1,0:T(8,128)(2,1)} %get-tuple-element.34.attended, ...), custom_call_target="tpu_custom_call" | custom-call | flops 12000000000 | bytes 16000000 | tf_op jit(solution)/shard_map/pallas_call | solution.py:340
  123.9 2.7 fusion.9
  127.3 1.0 copy-done.4
  128.3 12.5 %shard_map.247 = (bf16[256,768]{1,0:T(8,128)(2,1)}, bf16[256,3072]{1,0:T(8,128)(2,1)}, bf16[2,2,8,4,48,384]{5,4,3,2,1,0:T(8,128)(2,1)}, f32[1,3072]{1,0:T(1,128)}) custom-call(s32[2]{0:T(128)} %pad_add_fusion.place, bf16[256,768]{1,0:T(8,128)(2,1)} %cotangent.5, f32[256,3072]{1,0:T(8,128)} %get-tuple-element.35.hidden, ...), custom_call_target="tpu_custom_call" | custom-call | flops 12000000000 | bytes 16000000 | tf_op jit(solution)/shard_map/pallas_call | solution.py:357
  140.8 20.5 %shard_map.248 = (f32[256,768]{1,0:T(8,128)}, bf16[256,768]{1,0:T(8,128)(2,1)}, bf16[2,2,8,4,48,384]{5,4,3,2,1,0:T(8,128)(2,1)}, f32[8,768]{1,0:T(8,128)}) custom-call(s32[2]{0:T(128)} %pad_add_fusion.place, bf16[256,768]{1,0:T(8,128)(2,1)} %collective-permute-done.x_prev, bf16[256,768]{1,0:T(8,128)(2,1)} %x_here.5, bf16[256,768]{1,0:T(8,128)(2,1)} %cotangent.5, ...), custom_call_target="tpu_custom_call" | custom-call | flops 20000000000 | bytes 20000000 | tf_op jit(solution)/shard_map/pallas_call | solution.py:366
  161.3 5.1 %fusion.11 = (bf16[1,2,8,4,48,384]{5,4,3,2,1,0:T(8,128)(2,1)}, bf16[1,2,8,4,48,384]{5,4,3,2,1,0:T(8,128)(2,1)}) fusion(bf16[2,2,8,4,48,384]{5,4,3,2,1,0:T(8,128)(2,1)} %get-tuple-element.48), kind=kLoop, calls=%fused_computation.48 | loop fusion | bytes 9437184 | tf_op jit(solution)/shard_map/slice | solution.py:281
  166.4 2.0 fusion
  168.4 12.0 %all-to-all-start.4 = ((bf16[64,24,768]{2,1,0:T(8,128)(2,1)}), bf16[64,24,768]{2,1,0:T(8,128)(2,1)S(1)}, u32[]{:S(2)}, u32[]{:S(2)}) async-start(bf16[64,24,768]{2,1,0:T(8,128)(2,1)} %fusion), calls=%async_computation.4 | async-start | bytes 4718592 | tf_op jit(solution)/shard_map/all_to_all | solution.py:282
  180.4 5.2 %fusion.10 = (bf16[1,2,8,4,48,384]{5,4,3,2,1,0:T(8,128)(2,1)}, bf16[1,2,8,4,48,384]{5,4,3,2,1,0:T(8,128)(2,1)}) fusion(bf16[2,2,8,4,48,384]{5,4,3,2,1,0:T(8,128)(2,1)} %get-tuple-element.52), kind=kLoop, calls=%fused_computation.47 | loop fusion | bytes 9437184 | tf_op jit(solution)/shard_map/slice | solution.py:281
  185.8 3.7 fusion.2
  189.5 23.7 %all-to-all-done.4 = bf16[64,24,768]{2,1,0:T(8,128)(2,1)S(1)} async-done(((bf16[64,24,768]{2,1,0:T(8,128)(2,1)}), bf16[64,24,768]{2,1,0:T(8,128)(2,1)S(1)}, u32[]{:S(2)}, u32[]{:S(2)}) %all-to-all-start.4) | async-done | bytes 2359328 | tf_op jit(solution)/shard_map/all_to_all | solution.py:282
  213.2 5.9 %all-to-all-start = ((bf16[64,48,384]{2,1,0:T(8,128)(2,1)}), bf16[64,48,384]{2,1,0:T(8,128)(2,1)}, u32[]{:S(2)}, u32[]{:S(2)}) async-start(bf16[64,48,384]{2,1,0:T(8,128)(2,1)} %fusion.2), calls=%async_computation | async-start | bytes 4718592 | tf_op jit(solution)/shard_map/all_to_all | solution.py:282
  219.1 4.4 fusion.1
  223.4 26.7 %all-to-all-done = bf16[64,48,384]{2,1,0:T(8,128)(2,1)} async-done(((bf16[64,48,384]{2,1,0:T(8,128)(2,1)}), bf16[64,48,384]{2,1,0:T(8,128)(2,1)}, u32[]{:S(2)}, u32[]{:S(2)}) %all-to-all-start) | async-done | bytes 2359328 | tf_op jit(solution)/shard_map/all_to_all | solution.py:282
  250.2 7.3 %all-to-all-start.2 = ((bf16[64,48,384]{2,1,0:T(8,128)(2,1)}), bf16[64,48,384]{2,1,0:T(8,128)(2,1)}, u32[]{:S(2)}, u32[]{:S(2)}) async-start(bf16[64,48,384]{2,1,0:T(8,128)(2,1)} %fusion.1), calls=%async_computation.2 | async-start | bytes 4718592 | tf_op jit(solution)/shard_map/all_to_all | solution.py:282
  257.5 2.0 reduce_sum.36
  259.5 27.9 %all-to-all-done.2 = bf16[64,48,384]{2,1,0:T(8,128)(2,1)} async-done(((bf16[64,48,384]{2,1,0:T(8,128)(2,1)}), bf16[64,48,384]{2,1,0:T(8,128)(2,1)}, u32[]{:S(2)}, u32[]{:S(2)}) %all-to-all-start.2) | async-done | bytes 2359328 | tf_op jit(solution)/shard_map/all_to_all | solution.py:282
  287.4 1.1 broadcast_in_dim.50
  288.5 5.2 %all-to-all-start.1 = ((bf16[32,48,384]{2,1,0:T(8,128)(2,1)}), bf16[32,48,384]{2,1,0:T(8,128)(2,1)S(1)}, u32[]{:S(2)}, u32[]{:S(2)}) async-start(bf16[32,48,384]{2,1,0:T(8,128)(2,1)} %broadcast_in_dim.50), calls=%async_computation.1 | async-start | bytes 2359296 | tf_op jit(solution)/shard_map/all_to_all | solution.py:290
  294.7 16.4 %all-to-all-done.1 = bf16[32,48,384]{2,1,0:T(8,128)(2,1)S(1)} async-done(((bf16[32,48,384]{2,1,0:T(8,128)(2,1)}), bf16[32,48,384]{2,1,0:T(8,128)(2,1)S(1)}, u32[]{:S(2)}, u32[]{:S(2)}) %all-to-all-start.1) | async-done | bytes 1179680 | tf_op jit(solution)/shard_map/all_to_all | solution.py:290
  311.0 1.9 broadcast_in_dim.52
  312.9 3.9 all-to-all-start.5
  316.9 2.0 reduce_sum.37
  319.0 15.9 %all-to-all-done.5 = bf16[32,24,768]{2,1,0:T(8,128)(2,1)S(1)} async-done(((bf16[32,24,768]{2,1,0:T(8,128)(2,1)}), bf16[32,24,768]{2,1,0:T(8,128)(2,1)S(1)}, u32[]{:S(2)}, u32[]{:S(2)}) %all-to-all-start.5) | async-done | bytes 1179680 | tf_op jit(solution)/shard_map/all_to_all | solution.py:290
  334.8 1.1 broadcast_in_dim.51
  336.0 3.9 all-to-all-start.3
  339.9 1.3 collective-permute-start.10
  341.7 1.4 reduce.18
  343.7 1.4 pad_maximum_fusion.1
  345.1 73.8 %psum.7 = f32[12,768]{1,0:T(8,128)} all-reduce(f32[12,768]{1,0:T(8,128)} %pad_maximum_fusion.1), channel_id=1, replica_groups=mesh['x'=4,'z'=4,'y_lo'=2,'core'=2,'y_hi'=2] {'y_hi','x','z','y_lo','core'}, use_global_device_ids=true, to_apply=%region_1.2 | all-reduce | flops 9216 | bytes 73728 | tf_op jit(solution)/shard_map/psum | solution.py:380
  419.7 1.3 slice.155
  422.3 1.4 dynamic_slice.55
  424.4 1.0 fusion.12
  429.0 2.2 convert_add_fusion.3
  431.1 1.5 broadcast_select_fusion.3
  433.0 4.0 copy.28
  437.0 6.4 %reshape.102 = f32[384,3072]{1,0:T(8,128)} reshape(f32[8,48,2,4,384]{4,3,2,1,0:T(4,128)} %copy.28) | data formatting | bytes 9437184 | tf_op jit(solution)/shard_map/reshape | solution.py:386
  443.3 4.0 slice.154
  447.3 2.4 slice.156
  449.7 1.4 select_bitcast_fusion.1
  451.4 2.7 bitcast_convert_fusion
  454.1 1.5 broadcast_select_fusion.1
  455.9 4.0 copy.29
  459.8 6.4 %reshape.105 = f32[384,3072]{1,0:T(8,128)} reshape(f32[8,48,2,4,384]{4,3,2,1,0:T(4,128)} %copy.29) | data formatting | bytes 9437184 | tf_op jit(solution)/shard_map/reshape | solution.py:386
  (79 shorter events, 19.0 us)
Async XLA Ops:
  0.6 22.9 %copy-start.1 = (bf16[384,768]{1,0:T(8,128)(2,1)S(1)}, bf16[384,768]{1,0:T(8,128)(2,1)}, u32[]{:S(2)}) copy-start(bf16[384,768]{1,0:T(8,128)(2,1)} %out_own.3) | copy-start | bytes 1769476
  12.1 16.7 %collective-permute-start.3 = (bf16[4608]{0:T(1024)(128)(2,1)}, bf16[4608]{0:T(1024)(128)(2,1)S(1)}, u32[]{:S(2)}, u32[]{:S(2)}) collective-permute-start(bf16[4608]{0:T(1024)(128)(2,1)} %constant_dynamic-update-slice_fusion), channel_id=1, source_target_pairs={{0,1},{1,0},{2,3},{3,2},{4,5},{5,4},{6,7},{7,6},{8,9},{9,8},{10,11... | collective-permute-start | bytes 27656 | tf_op jit(solution)/shard_map/ppermute | solution.py:314
  16.6 29.7 %collective-permute-start.1 = (bf16[192,2304]{1,0:T(8,128)(2,1)S(1)}, bf16[192,2304]{1,0:T(8,128)(2,1)}, u32[]{:S(2)}, u32[]{:S(2)}) collective-permute-start(bf16[192,2304]{1,0:T(8,128)(2,1)S(1)} %constant_dynamic-slice_fusion.9), channel_id=1, source_target_pairs={{0,5},{1,4},{4,1},{5,0},{2,7},{3,6},{6,3},{7,2},{8,13},{9,12},{12,... | collective-permute-start | bytes 2654216 | tf_op jit(solution)/shard_map/ppermute | solution.py:274
  17.8 84.4 %collective-permute-start = (bf16[256,768]{1,0:T(8,128)(2,1)}, bf16[256,768]{1,0:T(8,128)(2,1)}, u32[]{:S(2)}, u32[]{:S(2)}) collective-permute-start(bf16[256,768]{1,0:T(8,128)(2,1)} %x_here.5), channel_id=1, source_target_pairs={{0,1},{2,3},{4,5},{6,7},{8,9},{10,11},{12,13},{14,15},{16,17},{18,... | collective-permute-start | bytes 1179656 | tf_op jit(solution)/shard_map/ppermute | solution.py:311
  23.4 48.1 %collective-permute-start.6 = (bf16[192,3072]{1,0:T(8,128)(2,1)S(1)}, bf16[192,3072]{1,0:T(8,128)(2,1)}, u32[]{:S(2)}, u32[]{:S(2)}) collective-permute-start(bf16[192,3072]{1,0:T(8,128)(2,1)S(1)} %constant_dynamic-slice_fusion.7), channel_id=1, source_target_pairs={{0,5},{1,4},{4,1},{5,0},{2,7},{3,6},{6,3},{7,2},{8,13},{9,12},{12,... | collective-permute-start | bytes 3538952 | tf_op jit(solution)/shard_map/ppermute | solution.py:274
  23.6 54.3 %collective-permute-start.4 = (bf16[192,768]{1,0:T(8,128)(2,1)S(1)}, bf16[192,768]{1,0:T(8,128)(2,1)}, u32[]{:S(2)}, u32[]{:S(2)}) collective-permute-start(bf16[192,768]{1,0:T(8,128)(2,1)S(1)} %constant_dynamic-slice_fusion.8), channel_id=1, source_target_pairs={{0,5},{1,4},{4,1},{5,0},{2,7},{3,6},{6,3},{7,2},{8,13},{9,12},{12,... | collective-permute-start | bytes 884744 | tf_op jit(solution)/shard_map/ppermute | solution.py:274
  28.8 72.9 %collective-permute-start.8 = (bf16[768,768]{1,0:T(8,128)(2,1)S(1)}, bf16[768,768]{1,0:T(8,128)(2,1)}, u32[]{:S(2)}, u32[]{:S(2)}) collective-permute-start(bf16[768,768]{1,0:T(8,128)(2,1)S(1)} %constant_dynamic-slice_fusion.6), channel_id=1, source_target_pairs={{0,5},{1,4},{4,1},{5,0},{2,7},{3,6},{6,3},{7,2},{8,13},{9,12},{12,... | collective-permute-start | bytes 3538952 | tf_op jit(solution)/shard_map/ppermute | solution.py:274
  46.3 55.9 %collective-permute-start.2 = (bf16[192,2304]{1,0:T(8,128)(2,1)}, bf16[192,2304]{1,0:T(8,128)(2,1)S(1)}, u32[]{:S(2)}, u32[]{:S(2)}) collective-permute-start(bf16[192,2304]{1,0:T(8,128)(2,1)} %collective-permute-done.1.near.qkv_near), channel_id=1, source_target_pairs={{0,2},{2,0},{1,3},{3,1},{4,6},{6,4},{5,7},{7,5},{8,10},{10,8},{9,1... | collective-permute-start | bytes 2654216 | tf_op jit(solution)/shard_map/ppermute | solution.py:275
  71.5 40.3 %collective-permute-start.7 = (bf16[192,3072]{1,0:T(8,128)(2,1)}, bf16[192,3072]{1,0:T(8,128)(2,1)S(1)}, u32[]{:S(2)}, u32[]{:S(2)}) collective-permute-start(bf16[192,3072]{1,0:T(8,128)(2,1)} %collective-permute-done.6.up_near), channel_id=1, source_target_pairs={{0,2},{2,0},{1,3},{3,1},{4,6},{6,4},{5,7},{7,5},{8,10},{10,8},{9,1... | collective-permute-start | bytes 3538952 | tf_op jit(solution)/shard_map/ppermute | solution.py:275
  77.9 34.0 %collective-permute-start.5 = (bf16[192,768]{1,0:T(8,128)(2,1)}, bf16[192,768]{1,0:T(8,128)(2,1)S(1)}, u32[]{:S(2)}, u32[]{:S(2)}) collective-permute-start(bf16[192,768]{1,0:T(8,128)(2,1)} %collective-permute-done.4.out_near), channel_id=1, source_target_pairs={{0,2},{2,0},{1,3},{3,1},{4,6},{6,4},{5,7},{7,5},{8,10},{10,8},{9,1... | collective-permute-start | bytes 884744 | tf_op jit(solution)/shard_map/ppermute | solution.py:275
  101.7 25.6 %collective-permute-start.9 = (bf16[768,768]{1,0:T(8,128)(2,1)}, bf16[768,768]{1,0:T(8,128)(2,1)S(1)}, u32[]{:S(2)}, u32[]{:S(2)}) collective-permute-start(bf16[768,768]{1,0:T(8,128)(2,1)} %collective-permute-done.8.near), channel_id=1, source_target_pairs={{0,2},{2,0},{1,3},{3,1},{4,6},{6,4},{5,7},{7,5},{8,10},{10,8},{9,1... | collective-permute-start | bytes 3538952 | tf_op jit(solution)/shard_map/ppermute | solution.py:275
  102.2 0.9 copy-start.5
  111.9 0.7 copy-start.6
  111.9 1.1 copy-start.3
  126.6 39.8 %collective-permute-start.15 = (bf16[64,24,768]{2,1,0:T(8,128)(2,1)S(1)}, bf16[64,24,768]{2,1,0:T(8,128)(2,1)S(1)}, u32[]{:S(2)}, u32[]{:S(2)}) collective-permute-start(bf16[64,24,768]{2,1,0:T(8,128)(2,1)S(1)} %bitcast.35), channel_id=1, source_target_pairs={{0,2},{2,0},{1,3},{3,1},{4,6},{6,4},{5,7},{7,5},{8,10},{10,8},{9,1... | collective-permute-start | bytes 7077896 | tf_op jit(solution)/shard_map/ppermute | solution.py:280
  127.3 1.0 copy-start.4
  166.3 19.5 %collective-permute-start.11 = (bf16[64,48,384]{2,1,0:T(8,128)(2,1)}, bf16[64,48,384]{2,1,0:T(8,128)(2,1)}, u32[]{:S(2)}, u32[]{:S(2)}) collective-permute-start(bf16[64,48,384]{2,1,0:T(8,128)(2,1)} %bitcast.4), channel_id=1, source_target_pairs={{0,2},{2,0},{1,3},{3,1},{4,6},{6,4},{5,7},{7,5},{8,10},{10,8},{9,1... | collective-permute-start | bytes 7077896 | tf_op jit(solution)/shard_map/ppermute | solution.py:280
  168.4 44.8 %all-to-all-start.4 = ((bf16[64,24,768]{2,1,0:T(8,128)(2,1)}), bf16[64,24,768]{2,1,0:T(8,128)(2,1)S(1)}, u32[]{:S(2)}, u32[]{:S(2)}) async-start(bf16[64,24,768]{2,1,0:T(8,128)(2,1)} %fusion), calls=%async_computation.4 | async-start | bytes 4718592 | tf_op jit(solution)/shard_map/all_to_all | solution.py:282
  180.4 5.4 %copy-start = (bf16[1,2,8,4,48,384]{5,4,3,2,1,0:T(8,128)(2,1)S(1)}, bf16[1,2,8,4,48,384]{5,4,3,2,1,0:T(8,128)(2,1)}, u32[]{:S(2)}) copy-start(bf16[1,2,8,4,48,384]{5,4,3,2,1,0:T(8,128)(2,1)} %get-tuple-element.58) | copy-start | bytes 7077892
  185.6 33.4 %collective-permute-start.13 = (bf16[64,48,384]{2,1,0:T(8,128)(2,1)}, bf16[64,48,384]{2,1,0:T(8,128)(2,1)}, u32[]{:S(2)}, u32[]{:S(2)}) collective-permute-start(bf16[64,48,384]{2,1,0:T(8,128)(2,1)} %bitcast.9), channel_id=1, source_target_pairs={{0,2},{2,0},{1,3},{3,1},{4,6},{6,4},{5,7},{7,5},{8,10},{10,8},{9,1... | collective-permute-start | bytes 7077896 | tf_op jit(solution)/shard_map/ppermute | solution.py:280
  213.2 37.0 %all-to-all-start = ((bf16[64,48,384]{2,1,0:T(8,128)(2,1)}), bf16[64,48,384]{2,1,0:T(8,128)(2,1)}, u32[]{:S(2)}, u32[]{:S(2)}) async-start(bf16[64,48,384]{2,1,0:T(8,128)(2,1)} %fusion.2), calls=%async_computation | async-start | bytes 4718592 | tf_op jit(solution)/shard_map/all_to_all | solution.py:282
  250.2 37.2 %all-to-all-start.2 = ((bf16[64,48,384]{2,1,0:T(8,128)(2,1)}), bf16[64,48,384]{2,1,0:T(8,128)(2,1)}, u32[]{:S(2)}, u32[]{:S(2)}) async-start(bf16[64,48,384]{2,1,0:T(8,128)(2,1)} %fusion.1), calls=%async_computation.2 | async-start | bytes 4718592 | tf_op jit(solution)/shard_map/all_to_all | solution.py:282
  288.5 22.5 %all-to-all-start.1 = ((bf16[32,48,384]{2,1,0:T(8,128)(2,1)}), bf16[32,48,384]{2,1,0:T(8,128)(2,1)S(1)}, u32[]{:S(2)}, u32[]{:S(2)}) async-start(bf16[32,48,384]{2,1,0:T(8,128)(2,1)} %broadcast_in_dim.50), calls=%async_computation.1 | async-start | bytes 2359296 | tf_op jit(solution)/shard_map/all_to_all | solution.py:290
  312.9 21.9 %all-to-all-start.5 = ((bf16[32,24,768]{2,1,0:T(8,128)(2,1)}), bf16[32,24,768]{2,1,0:T(8,128)(2,1)S(1)}, u32[]{:S(2)}, u32[]{:S(2)}) async-start(bf16[32,24,768]{2,1,0:T(8,128)(2,1)} %broadcast_in_dim.52), calls=%async_computation.5 | async-start | bytes 2359296 | tf_op jit(solution)/shard_map/all_to_all | solution.py:290
  316.8 114.3 %collective-permute-start.12 = (bf16[32,48,384]{2,1,0:T(8,128)(2,1)S(1)}, bf16[32,48,384]{2,1,0:T(8,128)(2,1)}, u32[]{:S(2)}, u32[]{:S(2)}) collective-permute-start(bf16[32,48,384]{2,1,0:T(8,128)(2,1)S(1)} %all-to-all-done.1), channel_id=1, source_target_pairs={{0,2},{2,0},{1,3},{3,1},{4,6},{6,4},{5,7},{7,5},{8,10},{10,8},{9,1... | collective-permute-start | bytes 3538952 | tf_op jit(solution)/shard_map/ppermute | solution.py:293
  319.0 24.8 %copy-start.2 = (f32[1,768]{1,0:T(1,128)S(1)}, f32[1,768]{1,0:T(1,128)}, u32[]{:S(2)}) copy-start(f32[1,768]{1,0:T(1,128)} %get-tuple-element.50) | copy-start | bytes 9220
  336.0 95.2 %all-to-all-start.3 = ((bf16[32,48,384]{2,1,0:T(8,128)(2,1)}), bf16[32,48,384]{2,1,0:T(8,128)(2,1)S(1)}, u32[]{:S(2)}, u32[]{:S(2)}) async-start(bf16[32,48,384]{2,1,0:T(8,128)(2,1)} %broadcast_in_dim.51), calls=%async_computation.3 | async-start | bytes 2359296 | tf_op jit(solution)/shard_map/all_to_all | solution.py:290
  339.9 89.0 %collective-permute-start.10 = (bf16[256,768]{1,0:T(8,128)(2,1)}, bf16[256,768]{1,0:T(8,128)(2,1)}, u32[]{:S(2)}, u32[]{:S(2)}) collective-permute-start(bf16[256,768]{1,0:T(8,128)(2,1)} %get-tuple-element.47), channel_id=1, source_target_pairs={{1,0},{3,2},{5,4},{7,6},{9,8},{11,10},{13,12},{15,14},{17,16},{19,... | collective-permute-start | bytes 1179656 | tf_op jit(solution)/shard_map/ppermute | solution.py:377
  343.7 106.0 %collective-permute-start.16 = (bf16[32,24,768]{2,1,0:T(8,128)(2,1)S(1)}, bf16[32,24,768]{2,1,0:T(8,128)(2,1)}, u32[]{:S(2)}, u32[]{:S(2)}) collective-permute-start(bf16[32,24,768]{2,1,0:T(8,128)(2,1)S(1)} %all-to-all-done.5), channel_id=1, source_target_pairs={{0,2},{2,0},{1,3},{3,1},{4,6},{6,4},{5,7},{7,5},{8,10},{10,8},{9,1... | collective-permute-start | bytes 3538952 | tf_op jit(solution)/shard_map/ppermute | solution.py:293
  431.1 22.9 %collective-permute-start.14 = (bf16[32,48,384]{2,1,0:T(8,128)(2,1)S(1)}, bf16[32,48,384]{2,1,0:T(8,128)(2,1)}, u32[]{:S(2)}, u32[]{:S(2)}) collective-permute-start(bf16[32,48,384]{2,1,0:T(8,128)(2,1)S(1)} %all-to-all-done.3), channel_id=1, source_target_pairs={{0,2},{2,0},{1,3},{3,1},{4,6},{6,4},{5,7},{7,5},{8,10},{10,8},{9,1... | collective-permute-start | bytes 3538952 | tf_op jit(solution)/shard_map/ppermute | solution.py:293
